TPU v7x, 256 devices: a whole 4x4x8 slice. The times are simulated.
256 devices in a mesh: chan: 64 (over z_hi, y, x), tm: 4 (over z_lo, core).
Axes of the slice: x: 4, y: 4, z: 8 (z_hi: 4, z_lo: 2; z = z_hi * 2 + z_lo), core: 2. Of those that a mesh axis runs over, the one named last changes fastest.
Arguments:
- records: bfloat16 [8192, 32, 1920], P('chan', 'tm'), may hold values from -6 to 6
- partners: int32 [64, 4], P('chan'), may hold values from -1 to 63, as said below
Outputs:
- stacked: float32 [64, 4, 128, 128], P('chan', None, 'tm')
Inputs may be any that keep to these rules, and one draw needn't show every extreme that they name: Each row b lists distinct partner blocks b + k with 1 <= k <= 4 in increasing order, then -1 in the remaining slots; the number of partners differs from block to block, row 0 has 4, every block but the last has at least one, the last none.
All inputs are finite; a program needn't handle non-finite values.
Results may differ from a plain program's by a relative error of at most 0.0058.
Values may be sent and summed in bfloat16 or wider, within the bound.
A program may use at most 128 MiB of HBM per device.

v0:
```python
import math

import jax
import jax.numpy as jnp
from jax import lax
from jax.sharding import PartitionSpec as P

FREQ = 768
LAGS = 128
REACH = 4


def passed_along(array, axis, by):
    count = lax.axis_size(axis)
    pairs = [(i, i + by) for i in range(count) if 0 <= i + by < count]
    return lax.ppermute(array, axis, pairs)


def make_forward(length, freq):
    times = jnp.arange(length, dtype=jnp.int32)[:, None]
    bins = jnp.arange(1, freq + 1, dtype=jnp.int32)[None, :]
    phase = times * bins % length
    angle = 2.0 * math.pi / length * phase.astype(jnp.float32)
    return jnp.concatenate([jnp.cos(angle), -jnp.sin(angle)], axis=1).astype(jnp.bfloat16)


def make_inverse(length, freq, lags):
    bins = jnp.arange(1, freq + 1, dtype=jnp.int32)[:, None]
    shifts = jnp.arange(lags, dtype=jnp.int32)[None, :] - lags // 2
    phase = bins * shifts % length
    angle = 2.0 * math.pi / length * phase.astype(jnp.float32)
    return jnp.concatenate([jnp.cos(angle), -jnp.sin(angle)], axis=0)


def whiten_local(records, forward, freq):
    channels, windows, length = records.shape
    spectrum = jnp.dot(records.reshape(-1, length), forward, preferred_element_type=jnp.float32)
    real_part = spectrum[:, :freq]
    imag_part = spectrum[:, freq:]
    magnitude = jnp.sqrt(real_part * real_part + imag_part * imag_part)
    water_level = jnp.mean(magnitude, axis=1, keepdims=True)
    denominator = magnitude + 0.1 * water_level + 1e-06
    whitened = jnp.concatenate([real_part / denominator, imag_part / denominator], axis=1)
    return whitened.astype(jnp.bfloat16).reshape(channels, windows, 2 * freq)


def cross_sum(left, right, freq):
    left = left.astype(jnp.float32)
    right = right.astype(jnp.float32)
    left_real, left_imag = (left[..., :freq], left[..., freq:])
    right_real, right_imag = (right[..., :freq], right[..., freq:])
    real_sum = jnp.sum(left_real * right_real + left_imag * right_imag, axis=1)
    imag_sum = jnp.sum(left_imag * right_real - left_real * right_imag, axis=1)
    return jnp.concatenate([real_sum, imag_sum], axis=1)


def body(records, partners):
    length = records.shape[2]
    forward = make_forward(length, FREQ)
    inverse = make_inverse(length, FREQ, LAGS)
    whitened = whiten_local(records, forward, FREQ)
    total_windows = records.shape[1] * lax.axis_size("tm")
    norm_scale = 1.0 / math.sqrt(total_windows * FREQ)
    crosses = []
    for offset in range(1, REACH + 1):
        arrived = passed_along(whitened, "chan", -offset)
        crosses.append(cross_sum(whitened, arrived, FREQ))
    crosses = jnp.stack(crosses)
    summed = lax.psum_scatter(crosses, "tm", scatter_dimension=1, tiled=True)
    lagged = (
        jnp.einsum("kcf,fl->kcl", summed, inverse, precision=lax.Precision.HIGHEST) * norm_scale
    )
    own_block = lax.axis_index("chan")
    offsets = partners[0] - own_block
    selector = (offsets[:, None] == jnp.arange(1, REACH + 1, dtype=jnp.int32)[None, :]).astype(
        jnp.float32
    )
    result = jnp.einsum("jk,kcl->jcl", selector, lagged, precision=lax.Precision.HIGHEST)
    return result[None]


def solution(mesh):
    return jax.shard_map(
        body,
        mesh=mesh,
        in_specs=(P("chan", "tm", None), P("chan", None)),
        out_specs=P("chan", None, "tm", None),
        check_vma=False,
    )
```

profile of v0, /device:TPU:95, one launch (start us, length us, event | category | flops | bytes accessed | tf_op | source)
XLA Modules:
  0.0 829.4 jit_solution(11209254147082551670)
XLA Ops:
  6.5 0.0 reduce-scatter.2.cloned.1.call-start
  6.5 0.0 copy-start
  6.5 24.9 %cosine_convert_fusion = (bf16[1920,768]{1,0:T(8,128)(2,1)S(1)}, bf16[1920,768]{1,0:T(8,128)(2,1)S(1)}) fusion(s32[768]{0:T(1024)S(1)} %iota_add_fusion), kind=kLoop, calls=%fused_computation.8 | loop fusion | flops 17694720 | bytes 5901312 | tf_op jit(solution)/shard_map/convert.4
  31.4 0.0 copy-done
  31.4 6.6 fusion.9
  38.1 1.2 fusion.33
  39.3 2.2 fusion.13
  41.5 1.0 fusion.32
  42.5 2.5 collective-permute-start
  44.9 2.7 collective-permute-start.1
  47.7 3.9 collective-permute-start.2
  51.6 2.3 collective-permute-start.3
  53.9 261.0 %collective-permute-done = bf16[128,8,1536]{2,1,0:T(8,128)(2,1)S(1)} collective-permute-done((bf16[128,8,1536]{2,1,0:T(8,128)(2,1)S(1)}, bf16[128,8,1536]{2,1,0:T(8,128)(2,1)S(1)}, u32[]{:S(2)}, u32[]{:S(2)}) %collective-permute-start) | collective-permute-done | bytes 3145760 | tf_op jit(solution)/shard_map/ppermute | solution.py:16
  314.9 3.5 convert_element_type.34
  318.4 0.0 collective-permute-done.1
  318.4 3.5 convert_element_type.35
  322.0 0.0 collective-permute-done.2
  322.0 3.5 convert_element_type.36
  325.4 0.0 collective-permute-done.3
  325.4 3.5 convert_element_type.37
  328.9 16.0 %add_reduce_fusion.3 = (f32[128,768]{1,0:T(8,128)S(1)}, f32[128,768]{1,0:T(8,128)}, f32[128,768]{1,0:T(8,128)}, f32[128,768]{1,0:T(8,128)}, f32[128,768]{1,0:T(8...) fusion(f32[128,8,1536]{2,1,0:T(8,128)} %convert_element_type.34, ...), kind=kLoop, calls=%fused_computation.24 | loop fusion | flops 24379392 | bytes 34603008 | tf_op jit(solution)/shard_map/reduce_sum | solution.py:52
  344.9 1.4 maximum_bitcast_fusion
  346.3 0.2 maximum_bitcast_fusion.2
  346.5 1.9 pad_maximum_fusion.1
  348.4 0.0 copy-start.1
  348.4 0.0 reduce-scatter.2.cloned.1.call-update
  348.4 0.6 copy-done.1
  349.0 1.7 fusion.22
  350.7 469.0 %reduce-scatter.2.cloned.1.call-done = f32[4,32,1536]{2,1,0:T(8,128)} async-done(((f32[4,128,1536]{2,1,0:T(8,128)}), f32[4,32,1536]{2,1,0:T(8,128)}) %reduce-scatter.2.cloned.1.call-update) | async-done | bytes 786448 | tf_op jit(solution)/shard_map/reduce_scatter | solution.py:69
  819.7 2.0 fusion.15
  821.7 0.3 convolution_bitcast_fusion
  822.0 0.6 copy.3
  (5 shorter events, 0.0 us)
Async XLA Ops:
  6.5 813.1 %reduce-scatter.2.cloned.1.call-start = ((), (), s32[]{:S(2)}) async-start(), calls=%async_computation.1 | async-start | bytes 3932160 | tf_op jit(solution)/shard_map/reduce_scatter | solution.py:69
  6.5 24.9 %copy-start = (bf16[128,8,1920]{2,1,0:T(8,128)(2,1)S(1)}, bf16[128,8,1920]{2,1,0:T(8,128)(2,1)}, u32[]{:S(2)}) copy-start(bf16[128,8,1920]{2,1,0:T(8,128)(2,1)} %param.2) | copy-start | bytes 11796484
  42.5 272.4 %collective-permute-start = (bf16[128,8,1536]{2,1,0:T(8,128)(2,1)S(1)}, bf16[128,8,1536]{2,1,0:T(8,128)(2,1)S(1)}, u32[]{:S(2)}, u32[]{:S(2)}) collective-permute-start(bf16[128,8,1536]{2,1,0:T(8,128)(2,1)S(1)} %get-tuple-element.24), channel_id=1, source_target_pairs={{4,0},{8,4},{12,8},{16,12},{20,16},{24,20},{28,24},{32,28},{36,32}... | collective-permute-start | bytes 9437192 | tf_op jit(solution)/shard_map/ppermute | solution.py:16
  44.9 273.5 %collective-permute-start.1 = (bf16[128,8,1536]{2,1,0:T(8,128)(2,1)S(1)}, bf16[128,8,1536]{2,1,0:T(8,128)(2,1)S(1)}, u32[]{:S(2)}, u32[]{:S(2)}) collective-permute-start(bf16[128,8,1536]{2,1,0:T(8,128)(2,1)S(1)} %get-tuple-element.24), channel_id=1, source_target_pairs={{8,0},{12,4},{16,8},{20,12},{24,16},{28,20},{32,24},{36,28},{40,32... | collective-permute-start | bytes 9437192 | tf_op jit(solution)/shard_map/ppermute | solution.py:16
  47.7 274.3 %collective-permute-start.2 = (bf16[128,8,1536]{2,1,0:T(8,128)(2,1)S(1)}, bf16[128,8,1536]{2,1,0:T(8,128)(2,1)S(1)}, u32[]{:S(2)}, u32[]{:S(2)}) collective-permute-start(bf16[128,8,1536]{2,1,0:T(8,128)(2,1)S(1)} %get-tuple-element.24), channel_id=1, source_target_pairs={{12,0},{16,4},{20,8},{24,12},{28,16},{32,20},{36,24},{40,28},{44,3... | collective-permute-start | bytes 9437192 | tf_op jit(solution)/shard_map/ppermute | solution.py:16
  51.6 273.8 %collective-permute-start.3 = (bf16[128,8,1536]{2,1,0:T(8,128)(2,1)S(1)}, bf16[128,8,1536]{2,1,0:T(8,128)(2,1)S(1)}, u32[]{:S(2)}, u32[]{:S(2)}) collective-permute-start(bf16[128,8,1536]{2,1,0:T(8,128)(2,1)S(1)} %get-tuple-element.24), channel_id=1, source_target_pairs={{16,0},{20,4},{24,8},{28,12},{32,16},{36,20},{40,24},{44,28},{48,3... | collective-permute-start | bytes 9437192 | tf_op jit(solution)/shard_map/ppermute | solution.py:16
  348.4 0.7 copy-start.1
Sparse Core Ops, SparseCore 0:
  348.5 471.1 reduce-scatter.1
where the time goes:
time: 832 us; the launch traced here: 829 us
  waiting for transfers between devices  730 us (88%)
  other arithmetic  64.4 us (8%)
  between operations  13.5 us (2%)
  starting transfers between devices  11.4 us (1%)
  matrix products  8.91 us (1%)
    reduce_scatter x1, waiting for transfers between devices, body(): summed = lax.psum_scatter(crosses, 'tm', scatter_dimension=1, tiled=True)  469 us
    ppermute x4, waiting for transfers between devices, passed_along(): return lax.ppermute(array, axis, pairs)  261 us
    another operation x1, other arithmetic  24.9 us
  transfers between devices with their start and end apart: 5, of which 2 were waited for; matrix products, arithmetic and copies ran while one was open for 1% of the time, Pallas kernels for 0%

commit v1 on v0

v1 whole, which is shorter than its diff:
```python
import functools
import math

import jax
import jax.numpy as jnp
import numpy as np
from jax import lax
from jax.experimental import pallas as pl
from jax.experimental.pallas import tpu as pltpu
from jax.sharding import PartitionSpec as P

FREQ = 768
LAGS = 128
REACH = 4
LEN = 1920
ROW = 4
TM = 4
CHUNKS = 8
PIECES = 3
WIDE = FREQ // PIECES
MESH = pl.DeviceIdType.MESH
F32 = jnp.float32
BF16 = jnp.bfloat16


def forward_matrix():
    times = np.arange(LEN, dtype=np.int64)[:, None]
    bins = np.arange(1, FREQ + 1, dtype=np.int64)[None, :]
    angle = 2.0 * math.pi / LEN * (times * bins % LEN)
    real, imag = np.cos(angle), -np.sin(angle)
    pieces = [
        np.concatenate([real[:, p * WIDE : (p + 1) * WIDE], imag[:, p * WIDE : (p + 1) * WIDE]], 1)
        for p in range(PIECES)
    ]
    return np.stack(pieces).astype(np.float32).astype(BF16)


def inverse_matrix():
    bins = np.arange(1, FREQ + 1, dtype=np.int64)[:, None]
    shifts = np.arange(LAGS, dtype=np.int64)[None, :] - LAGS // 2
    angle = 2.0 * math.pi / LEN * (bins * shifts % LEN)
    whole = np.concatenate([np.cos(angle), -np.sin(angle)], 0).astype(np.float32)
    high = whole.astype(BF16)
    low = (whole - high.astype(np.float32)).astype(BF16)
    return np.concatenate([high, low], 1)


def gather_rows(tiles, sub):
    for shift in (1, 2, 4):
        mask = (sub & shift) == 0
        tiles = [
            jnp.where(mask, a, b) + pltpu.roll(jnp.where(mask, b, a), 8 - shift, 0)
            for a, b in zip(tiles[::2], tiles[1::2])
        ]
    return tiles[0]


def kernel(
    scale, rec_hbm, fwd_hbm, inv_hbm, out_ref,
    rec, fwd, inv, own, held, down, up, cross, lag, from_row, from_next,
    rec_sem, fwd_sem, inv_sem, xs_sem, xr_sem, ys_sem, yr_sem, os_sem, or_sem,
):
    chan, tm = lax.axis_index("chan"), lax.axis_index("tm")
    x, row = lax.rem(chan, ROW), chan // ROW
    rows = lax.axis_size("chan") // ROW
    row_before, row_after = lax.rem(row + rows - 1, rows), lax.rem(row + 1, rows)

    def fwd_copy(p):
        return pltpu.make_async_copy(fwd_hbm.at[p], fwd.at[p], fwd_sem.at[p])

    def rec_copy(k):
        return pltpu.make_async_copy(rec_hbm.at[:, pl.ds(4 * k, 4)], rec.at[k], rec_sem.at[k])

    rec_copy(0).start()
    for p in range(PIECES):
        fwd_copy(p).start()
    inv_copy = pltpu.make_async_copy(inv_hbm, inv, inv_sem)
    inv_copy.start()

    @pl.loop(1, CHUNKS)
    def _(k):
        rec_copy(k).start()

    barrier = pltpu.get_barrier_semaphore()

    def greet(there):
        pl.semaphore_signal(barrier, inc=1, device_id=there, device_id_type=MESH)

    for d in range(1, ROW):
        greet((row * ROW + lax.rem(x + d, ROW), tm))
    greet((row_before * ROW + x, tm))
    greet((row_after * ROW + x, tm))
    for t in range(TM):

        @pl.when(jnp.logical_or(x != tm, tm != t))
        def _():
            greet((row * ROW + tm, t))

        greet((row_after * ROW + tm, t))
    peers = ROW - 1 + 2 + TM + TM

    @pl.when(x != tm)
    def _():
        pl.semaphore_wait(barrier, peers)

    @pl.when(x == tm)
    def _():
        pl.semaphore_wait(barrier, peers - 1)

    def x_send(k, d):
        there = lax.rem(x + d, ROW)
        return pltpu.make_async_remote_copy(
            src_ref=own.at[there, k], dst_ref=held.at[k, :, x],
            send_sem=xs_sem.at[k, d - 1], recv_sem=xr_sem.at[k, d - 1],
            device_id=(row * ROW + there, tm), device_id_type=MESH,
        )

    def down_send(k):
        return pltpu.make_async_remote_copy(
            src_ref=held.at[k, 0], dst_ref=down.at[k],
            send_sem=ys_sem.at[k, 0], recv_sem=yr_sem.at[k, 0],
            device_id=(row_before * ROW + x, tm), device_id_type=MESH,
        )

    def up_send(k):
        return pltpu.make_async_remote_copy(
            src_ref=held.at[k, 1], dst_ref=up.at[k],
            send_sem=ys_sem.at[k, 1], recv_sem=yr_sem.at[k, 1],
            device_id=(row_after * ROW + x, tm), device_id_type=MESH,
        )

    def row_result(i):
        return pltpu.make_async_remote_copy(
            src_ref=lag.at[i], dst_ref=from_row.at[tm],
            send_sem=os_sem.at[i, 0], recv_sem=or_sem.at[tm, 0],
            device_id=(row * ROW + i, x), device_id_type=MESH,
        )

    def next_result(i):
        return pltpu.make_async_remote_copy(
            src_ref=lag.at[i, 1], dst_ref=from_next.at[tm],
            send_sem=os_sem.at[i, 1], recv_sem=or_sem.at[tm, 1],
            device_id=(row_before * ROW + i, x), device_id_type=MESH,
        )

    def whiten(k):
        rec_copy(k).wait()
        data = rec[k].reshape(128, LEN)
        reals, imags, mags = [], [], []
        for p in range(PIECES):

            @pl.when(k == 0)
            def _():
                fwd_copy(p).wait()

            spectrum = jnp.dot(data, fwd[p], preferred_element_type=F32)
            real, imag = spectrum[:, :WIDE], spectrum[:, WIDE:]
            reals.append(real)
            imags.append(imag)
            mags.append(jnp.sqrt(real * real + imag * imag))
        total = sum(jnp.sum(mag, axis=1, keepdims=True) for mag in mags)
        floor = 0.1 * (total * (1.0 / FREQ)) + 1e-06
        for p in range(PIECES):
            inverse = 1.0 / (mags[p] + floor)
            for at, part in ((p * WIDE, reals[p]), (FREQ + p * WIDE, imags[p])):
                white = (part * inverse).astype(BF16).reshape(ROW, 2, 16, WIDE)
                for there in range(ROW):
                    own[there, k, :, :, at : at + WIDE] = white[there]
        held[k, :, x] = own[x, k]

    sub = lax.broadcasted_iota(jnp.int32, (8, 128), 0)

    def correlate(k):
        @pl.loop(0, FREQ // 128)
        def _(tile):
            real_at = pl.ds(pl.multiple_of(tile * 128, 128), 128)
            imag_at = pl.ds(pl.multiple_of(FREQ + tile * 128, 128), 128)

            def load(ref, *at):
                real = ref[*at, :, real_at].astype(F32)
                imag = ref[*at, :, imag_at].astype(F32)
                return [(real[c * 8 : c * 8 + 8], imag[c * 8 : c * 8 + 8]) for c in range(2)]

            for half in range(2):
                here = [load(held, k, half, i) for i in range(ROW)]
                other = [load(down if half == 0 else up, k, i) for i in range(ROW)]
                for i in range(ROW):
                    real_tiles, imag_tiles = [], []
                    for offset in range(1, REACH + 1):
                        q = i + offset
                        if q < ROW:
                            left, right = here[i], here[q]
                        elif half == 0:
                            left, right = here[i], other[q - ROW]
                        else:
                            left, right = other[i], here[q - ROW]
                        for (ar, ai), (pr, pi) in zip(left, right):
                            real_tiles.append(ar * pr + ai * pi)
                            imag_tiles.append(ai * pr - ar * pi)
                    at = pl.ds((half * ROW + i) * 8, 8)
                    cross[at, real_at] = gather_rows(real_tiles, sub)
                    cross[at, imag_at] = gather_rows(imag_tiles, sub)

        whole = cross[...]
        high = whole.astype(BF16)
        low = (whole - high.astype(F32)).astype(BF16)
        first = jnp.dot(high, inv[...], preferred_element_type=F32)
        second = jnp.dot(low, inv[:, :LAGS], preferred_element_type=F32)
        lagged = (first[:, :LAGS] + (first[:, LAGS:] + second)) * scale
        for half in range(2):
            for i in range(ROW):
                at = (half * ROW + i) * 8
                lag[i, half, k] = lagged[at : at + 8]

    inv_copy.wait()

    @pl.loop(0, CHUNKS + 2)
    def _(step):
        @pl.when(step < CHUNKS)
        def _():
            whiten(step)
            for d in (2, 1, 3):
                x_send(step, d).start()

        @pl.when(jnp.logical_and(step >= 1, step < CHUNKS + 1))
        def _():
            k = step - 1
            for d in range(1, ROW):
                x_send(k, d).wait_recv()
            down_send(k).start()
            up_send(k).start()

        @pl.when(step >= 2)
        def _():
            k = step - 2
            down_send(k).wait_recv()
            up_send(k).wait_recv()
            correlate(k)

    for i in range(ROW):

        @pl.when(jnp.logical_or(x != tm, x != i))
        def _():
            row_result(i).start()

        @pl.when(jnp.logical_and(x == tm, x == i))
        def _():
            from_row[tm] = lag[i]

        next_result(i).start()

    @pl.loop(0, CHUNKS)
    def _(k):
        for d in range(1, ROW):
            x_send(k, d).wait_send()
        down_send(k).wait_send()
        up_send(k).wait_send()

    for i in range(ROW):

        @pl.when(jnp.logical_or(x != tm, x != i))
        def _():
            row_result(i).wait_send()

        next_result(i).wait_send()

    for t in range(TM):

        @pl.when(jnp.logical_or(x != tm, tm != t))
        def _():
            pltpu.make_async_remote_copy(
                src_ref=lag.at[0], dst_ref=from_row.at[t], send_sem=os_sem.at[0, 0],
                recv_sem=or_sem.at[t, 0], device_id=(row * ROW + tm, t), device_id_type=MESH,
            ).wait_recv()

        pltpu.make_async_remote_copy(
            src_ref=lag.at[0, 1], dst_ref=from_next.at[t], send_sem=os_sem.at[0, 1],
            recv_sem=or_sem.at[t, 1], device_id=(row_after * ROW + tm, t), device_id_type=MESH,
        ).wait_recv()

    inside = sub // 2 + 1 <= ROW - 1 - x
    for k in range(CHUNKS):
        out_ref[0, k] = (from_row[0, 0, k] + from_row[1, 0, k]) + (
            from_row[2, 0, k] + from_row[3, 0, k]
        )
        within = (from_row[0, 1, k] + from_row[1, 1, k]) + (
            from_row[2, 1, k] + from_row[3, 1, k]
        )
        across = (from_next[0, k] + from_next[1, k]) + (from_next[2, k] + from_next[3, k])
        out_ref[1, k] = jnp.where(inside, within, across)


def body(records, partners):
    channels, windows, length = records.shape
    total_windows = windows * lax.axis_size("tm")
    scale = 1.0 / math.sqrt(total_windows * FREQ)
    dma = pltpu.SemaphoreType.DMA
    result = pl.pallas_call(
        functools.partial(kernel, scale),
        out_shape=jax.ShapeDtypeStruct((2, CHUNKS, 8, LAGS), F32),
        in_specs=[pl.BlockSpec(memory_space=pl.ANY)] * 3,
        out_specs=pl.BlockSpec(memory_space=pltpu.VMEM),
        scratch_shapes=[
            pltpu.VMEM((CHUNKS, ROW, 4, windows, length), BF16),
            pltpu.VMEM((PIECES, LEN, 2 * WIDE), BF16),
            pltpu.VMEM((2 * FREQ, 2 * LAGS), BF16),
            pltpu.VMEM((ROW, CHUNKS, 2, 16, 2 * FREQ), BF16),
            pltpu.VMEM((CHUNKS, 2, ROW, 16, 2 * FREQ), BF16),
            pltpu.VMEM((CHUNKS, ROW, 16, 2 * FREQ), BF16),
            pltpu.VMEM((CHUNKS, ROW, 16, 2 * FREQ), BF16),
            pltpu.VMEM((64, 2 * FREQ), F32),
            pltpu.VMEM((ROW, 2, CHUNKS, 8, LAGS), F32),
            pltpu.VMEM((TM, 2, CHUNKS, 8, LAGS), F32),
            pltpu.VMEM((TM, CHUNKS, 8, LAGS), F32),
            dma((CHUNKS,)), dma((PIECES,)), dma,
            dma((CHUNKS, 3)), dma((CHUNKS, 3)),
            dma((CHUNKS, 2)), dma((CHUNKS, 2)),
            dma((ROW, 2)), dma((TM, 2)),
        ],
        compiler_params=pltpu.CompilerParams(
            collective_id=0, has_side_effects=True, vmem_limit_bytes=56 << 20
        ),
        cost_estimate=pl.CostEstimate(
            flops=7 * 10**9, bytes_accessed=12 * 10**6, transcendentals=10**6
        ),
    )(
        records.reshape(ROW, channels // ROW, windows, length),
        jnp.asarray(forward_matrix()),
        jnp.asarray(inverse_matrix()),
    )
    result = result.reshape(2, CHUNKS, REACH, 2, LAGS)
    lagged = result.transpose(2, 1, 0, 3, 4).reshape(REACH, channels // TM, LAGS)
    offsets = partners[0] - lax.axis_index("chan")
    chosen = 0.0
    for k in range(REACH):
        chosen = chosen + jnp.where((offsets == k + 1)[:, None, None], lagged[k][None], 0.0)
    return chosen[None]


def solution(mesh):
    return jax.shard_map(
        body,
        mesh=mesh,
        in_specs=(P("chan", "tm", None), P("chan", None)),
        out_specs=P("chan", None, "tm", None),
        check_vma=False,
    )
```

time: 832 us -> 110 us (0.13)
  waiting for transfers between devices: 730 us -> 0 us
  Pallas kernels: 0 us -> 106 us
  other arithmetic: 64.4 us -> 0.74 us
  between operations: 13.5 us -> 0.05 us
  starting transfers between devices: 11.4 us -> 0 us
  matrix products: 8.91 us -> 0 us
    reduce_scatter x1 -> x0, waiting for transfers between devices: 469 us -> none  [body(): summed = lax.psum_scatter(crosses, 'tm', scatter_dimension=1, tiled=True)]
    ppermute x4 -> x0, waiting for transfers between devices: 261 us -> none  [passed_along(): return lax.ppermute(array, axis, pairs)]
    pallas_call x0 -> x1, Pallas kernels: none -> 106 us  [body(): pl.pallas_call(functools.partial(kernel, scale), out_shape=jax.ShapeDtype...]
    another operation x4 -> x0, other arithmetic: 28.3 us -> none
    reduce_sum x2 -> x0, other arithmetic: 17.1 us -> none  [the longest x1 16 us: cross_sum(): real_sum = jnp.sum(left_real * right_real + left_imag * right_imag, axis=1)]
    convert_element_type x5 -> x0, other arithmetic: 15 us -> none  [the longest x4 14 us: cross_sum(): right = right.astype(jnp.float32)]
    ppermute x4 -> x0, starting transfers between devices: 11.4 us -> none  [passed_along(): return lax.ppermute(array, axis, pairs)]
    dot_general x3 -> x0, matrix products: 8.91 us -> none  [the longest x1 6.64 us: whiten_local(): jnp.dot(records.reshape(-1, length), forward, preferred_element_type=jnp....]
  transfers between devices with their start and end apart: 5 -> 0, of which waited for: 2 -> 0; matrix products, arithmetic and copies ran while one was open for 1% -> 0% of each run, Pallas kernels for 0% -> 0%
where the time goes in v1:
time: 110 us; the launch traced here: 108 us
  Pallas kernels  106 us (96%)
    pallas_call x1, Pallas kernels, body(): pl.pallas_call(functools.partial(kernel, scale), out_shape=jax.ShapeDtype...  106 us

profile of v1, /device:TPU:95, one launch (start us, length us, event | category | flops | bytes accessed | tf_op | source)
XLA Modules:
  0.0 107.7 jit_solution(10396228889234748849)
XLA Ops:
  0.0 0.0 copy-start
  0.0 106.1 %shard_map.46 = f32[2,8,8,128]{3,2,1,0:T(8,128)} custom-call(bf16[4,32,8,1920]{3,2,1,0:T(8,128)(2,1)} %bitcast.23, bf16[3,1920,512]{2,1,0:T(8,128)(2,1)} %constant.20.clone.fwd_hbm, bf16[1536,256]{1,0:T(8,128)(2,1)} %constant.21.clone.inv_hbm), custom_call_target="tpu_custom_call" | custom-call | flops 7000000000 | bytes 12000000 | tf_op jit(solution)/shard_map/pallas_call | solution.py:298
  106.1 0.9 copy.7
  107.0 0.0 copy-done
  107.0 0.7 select_add_fusion
  (3 shorter events, 0.0 us)
Async XLA Ops:
  0.0 107.0 %copy-start = (s32[1,4]{1,0:T(1,128)S(1)}, s32[1,4]{1,0:T(1,128)}, u32[]{:S(2)}) copy-start(s32[1,4]{1,0:T(1,128)} %param.5) | copy-start | bytes 52

commit v2 on v1

v2 whole, which is shorter than its diff:
```python
import functools
import math

import jax
import jax.numpy as jnp
import numpy as np
from jax import lax
from jax.experimental import pallas as pl
from jax.experimental.pallas import tpu as pltpu
from jax.sharding import PartitionSpec as P

FREQ = 768
LAGS = 128
REACH = 4
LEN = 1920
ROW = 4
TM = 4
CHUNKS = 4
PIECES = 3
UNITS = CHUNKS * PIECES
PASS, USE = 1, 4
WIDE = FREQ // PIECES
MESH = pl.DeviceIdType.MESH
F32 = jnp.float32
BF16 = jnp.bfloat16
RESULT = jnp.bfloat16


def forward_matrix():
    times = np.arange(LEN, dtype=np.int64)[:, None]
    bins = np.arange(1, FREQ + 1, dtype=np.int64)[None, :]
    angle = 2.0 * math.pi / LEN * (times * bins % LEN)
    real, imag = np.cos(angle), -np.sin(angle)
    pieces = [
        np.concatenate([real[:, p * WIDE : (p + 1) * WIDE], imag[:, p * WIDE : (p + 1) * WIDE]], 1)
        for p in range(PIECES)
    ]
    return np.stack(pieces).astype(np.float32).astype(BF16)


def inverse_matrix():
    bins = np.arange(1, FREQ + 1, dtype=np.int64)[:, None]
    shifts = np.arange(LAGS, dtype=np.int64)[None, :] - LAGS // 2
    angle = 2.0 * math.pi / LEN * (bins * shifts % LEN)
    whole = np.concatenate([np.cos(angle), -np.sin(angle)], 0).astype(np.float32)
    high = whole.astype(BF16)
    low = (whole - high.astype(np.float32)).astype(BF16)
    both = np.concatenate([high, low], 1).reshape(2, PIECES, WIDE, 2 * LAGS)
    return both.transpose(1, 0, 2, 3).reshape(PIECES, 2 * WIDE, 2 * LAGS)


def gather_rows(tiles, sub):
    for shift in (1, 2, 4):
        mask = (sub & shift) == 0
        tiles = [
            jnp.where(mask, a, b) + pltpu.roll(jnp.where(mask, b, a), 8 - shift, 0)
            for a, b in zip(tiles[::2], tiles[1::2])
        ]
    return tiles[0]


def kernel(
    scale, rec_hbm, fwd_hbm, inv_hbm, out_ref,
    rec, fwd, inv, own, held, down, up, relay, cross, total, mine, mates, lag, from_row, from_next,
    rec_sem, fwd_sem, inv_sem, xs_sem, xr_sem, ys_sem, yr_sem, rs_sem, rr_sem, ms_sem, mr_sem, os_sem, or_sem,
):
    chan, tm = lax.axis_index("chan"), lax.axis_index("tm")
    rows = lax.axis_size("chan") // ROW
    planes = rows // ROW
    x, row = lax.rem(chan, ROW), chan // ROW
    y, plane = lax.rem(row, ROW), row // ROW
    has_before, has_after = row > 0, row < rows - 1
    core, pair = lax.rem(tm, 2), tm // 2
    mate = tm + 1 - 2 * core
    sums = lax.rem(x + tm, 2) == 0
    first, last = y == 0, y == ROW - 1
    passes_down = jnp.logical_and(last, plane > 0)
    passes_up = jnp.logical_and(first, plane < planes - 1)

    def device(by, at=x):
        return lax.rem(row + rows + by, rows) * ROW + at

    def fwd_copy(p):
        return pltpu.make_async_copy(fwd_hbm.at[p], fwd.at[p], fwd_sem.at[p])

    def rec_copy(c):
        return pltpu.make_async_copy(rec_hbm.at[:, c], rec.at[c], rec_sem.at[c])

    rec_copy(0).start()
    for p in range(PIECES):
        fwd_copy(p).start()
    inv_copy = pltpu.make_async_copy(inv_hbm, inv, inv_sem)
    inv_copy.start()
    for c in range(1, CHUNKS):
        rec_copy(c).start()

    from_next[...] = jnp.zeros(from_next.shape, from_next.dtype)
    barrier = pltpu.get_barrier_semaphore()

    def greet(*there):
        pl.semaphore_signal(barrier, inc=1, device_id=there, device_id_type=MESH)

    for d in range(1, ROW):
        greet(device(0, lax.rem(x + d, ROW)), tm)
    for t in range(TM // 2):

        @pl.when(jnp.logical_or(x != tm, pair != t))
        def _():
            greet(device(0, tm), 2 * t + core)

    @pl.when(sums)
    def _():
        greet(chan, mate)

    @pl.when(has_before)
    def _():
        greet(device(-1), tm)

        @pl.when(first)
        def _():
            greet(device(-ROW), tm)

    @pl.when(has_after)
    def _():
        greet(device(1), tm)
        for t in range(TM // 2):
            greet(device(1, tm), 2 * t + core)

        @pl.when(last)
        def _():
            greet(device(ROW), tm)

    @pl.when(passes_up)
    def _():
        greet(device(ROW - 1), tm)

    @pl.when(passes_down)
    def _():
        greet(device(1 - ROW), tm)

    itself = 1 - ((x - tm) * (x - tm) + 15) // 16
    before, after = (row + rows - 1) // rows, 1 - (row + 1) // rows
    edge = ((2 * y - 3) * (2 * y - 3)) // 9
    around = (plane + planes - 1) // planes + 1 - (plane + 1) // planes
    other = lax.rem(x + tm, 2)
    results = other + (1 - other) * (ROW - itself + ROW * before)
    peers = ROW - 1 + results + before + after + edge * around

    def x_send(u, half, d):
        c, p = u // PIECES, lax.rem(u, PIECES)
        there = lax.rem(x + d, ROW)
        return pltpu.make_async_remote_copy(
            src_ref=own.at[there, c, p, half], dst_ref=held.at[c, p, half, x],
            send_sem=xs_sem.at[u, half, d - 1], recv_sem=xr_sem.at[u, half, d - 1],
            device_id=(device(0, there), tm), device_id_type=MESH,
        )

    def straight(u, half, part):
        c, p = u // PIECES, lax.rem(u, PIECES)
        at = pl.ds(2 * part, 2)
        return pltpu.make_async_remote_copy(
            src_ref=held.at[c, p, half, at], dst_ref=(up if half else down).at[c, p, at],
            send_sem=ys_sem.at[u, half, part], recv_sem=yr_sem.at[u, half, part],
            device_id=(device(1 if half else -1), tm), device_id_type=MESH,
        )

    def detour(u, half):
        c, p = u // PIECES, lax.rem(u, PIECES)
        return pltpu.make_async_remote_copy(
            src_ref=held.at[c, p, half, pl.ds(2, 2)], dst_ref=relay.at[c, p],
            send_sem=ys_sem.at[u, half, 1], recv_sem=rr_sem.at[u],
            device_id=(device(1 - ROW if half else ROW - 1), tm), device_id_type=MESH,
        )

    def passed_on(u, half):
        c, p = u // PIECES, lax.rem(u, PIECES)
        return pltpu.make_async_remote_copy(
            src_ref=relay.at[c, p], dst_ref=(up if half else down).at[c, p, pl.ds(2, 2)],
            send_sem=rs_sem.at[u], recv_sem=yr_sem.at[u, half, 1],
            device_id=(device(ROW if half else -ROW), tm), device_id_type=MESH,
        )

    sends = ((0, has_before, first), (1, has_after, last))
    passes = ((0, passes_down), (1, passes_up))

    def halo_start(u):
        for half, wanted, at_edge in sends:

            @pl.when(jnp.logical_and(wanted, at_edge))
            def _():
                detour(u, half).start()

        for half, wanted, at_edge in sends:

            @pl.when(wanted)
            def _():
                straight(u, half, 0).start()

            @pl.when(jnp.logical_and(wanted, jnp.logical_not(at_edge)))
            def _():
                straight(u, half, 1).start()

    def pass_on(u):
        for half, wanted in passes:

            @pl.when(wanted)
            def _():
                detour(u, half).wait_recv()
                passed_on(u, half).start()

    def halo_arrived(u):
        for half, wanted in ((0, has_after), (1, has_before)):

            @pl.when(wanted)
            def _():
                for part in range(2):
                    straight(u, half, part).wait_recv()

    def halo_sent(u):
        for half, wanted, _ in sends:

            @pl.when(wanted)
            def _():
                for part in range(2):
                    straight(u, half, part).wait_send()

        for half, wanted in passes:

            @pl.when(wanted)
            def _():
                passed_on(u, half).wait_send()

    def mate_send(c):
        return pltpu.make_async_remote_copy(
            src_ref=mine.at[c], dst_ref=mates.at[c],
            send_sem=ms_sem.at[c], recv_sem=mr_sem.at[c],
            device_id=(chan, mate), device_id_type=MESH,
        )

    def row_result(c, i, t):
        return pltpu.make_async_remote_copy(
            src_ref=lag.at[i, c], dst_ref=from_row.at[t, c],
            send_sem=os_sem.at[i, c, 0], recv_sem=or_sem.at[t, c, 0],
            device_id=(device(0, i), x), device_id_type=MESH,
        )

    def next_result(c, i, t):
        at = pl.ds(16, 16) if i < 2 else pl.ds(0, 32)
        return pltpu.make_async_remote_copy(
            src_ref=lag.at[i, c, at], dst_ref=from_next.at[t, c, at],
            send_sem=os_sem.at[i, c, 1], recv_sem=or_sem.at[t, c, 1],
            device_id=(device(-1, i), x), device_id_type=MESH,
        )

    def whiten(c, half):
        @pl.when(half == 0)
        def _():
            rec_copy(c).wait()

        data = rec[c, :, half].reshape(128, LEN)
        reals, imags, mags = [], [], []
        for p in range(PIECES):
            if isinstance(c, int) and c == 0 and half == 0:
                fwd_copy(p).wait()
            spectrum = jnp.dot(data, fwd[p], preferred_element_type=F32)
            real, imag = spectrum[:, :WIDE], spectrum[:, WIDE:]
            reals.append(real)
            imags.append(imag)
            mags.append(jnp.sqrt(real * real + imag * imag))
        water = sum(jnp.sum(mag, axis=1, keepdims=True) for mag in mags) * (1.0 / FREQ)
        floor = 0.1 * water + 1e-06
        for p in range(PIECES):
            inverse = 1.0 / (mags[p] + floor)
            for at, part in ((0, reals[p]), (WIDE, imags[p])):
                white = (part * inverse).astype(BF16).reshape(ROW, 32, WIDE)
                for there in range(ROW):
                    own[there, c, p, half, :, at : at + WIDE] = white[there]
        for p in range(PIECES):
            held[c, p, half, x] = own[x, c, p, half]

    sub = lax.broadcasted_iota(jnp.int32, (8, 128), 0)

    def correlate(c, p):
        for lane in range(0, WIDE, 128):

            def load(ref, *at):
                both = []
                for lanes in (lane, WIDE + lane):
                    part = ref[*at, :, lanes : lanes + 128].astype(F32)
                    both.append([part[8 * n : 8 * n + 8] for n in range(4)])
                return list(zip(*both))

            here = [[load(held, c, p, half, i) for i in range(ROW)] for half in range(2)]
            after = [load(down, c, p, i) for i in range(ROW)]
            before = [load(up, c, p, i) for i in range(ROW)]
            for i in range(ROW):
                for offset in range(1, REACH + 1):
                    q = i + offset
                    if q < ROW:
                        lefts = here[0][i] + here[1][i]
                        rights = here[0][q] + here[1][q]
                    else:
                        lefts = here[0][i] + before[i]
                        rights = after[q - ROW] + here[1][q - ROW]
                    pairs = list(zip(lefts, rights))
                    reals = [ar * pr + ai * pi for (ar, ai), (pr, pi) in pairs]
                    imags = [ai * pr - ar * pi for (ar, ai), (pr, pi) in pairs]
                    at = (i * REACH + offset - 1) * 8
                    cross[at : at + 8, lane : lane + 128] = gather_rows(reals, sub)
                    cross[at : at + 8, WIDE + lane : WIDE + lane + 128] = gather_rows(imags, sub)

        whole = cross[...]
        high = whole.astype(BF16)
        low = (whole - high.astype(F32)).astype(BF16)
        first = jnp.dot(high, inv[p], preferred_element_type=F32)
        second = jnp.dot(low, inv[p, :, :LAGS], preferred_element_type=F32)
        term = first[:, :LAGS] + (first[:, LAGS:] + second)

        @pl.when(p == 0)
        def _():
            total[...] = term

        @pl.when(p > 0)
        def _():
            total[...] += term

    def keep_results(c):
        mine[c] = total[...] * scale

        @pl.when(jnp.logical_not(sums))
        def _():
            mate_send(c).start()

    def send_results(c):
        @pl.when(sums)
        def _():
            mate_send(c).wait_recv()
            for i in range(ROW):
                at = pl.ds(32 * i, 32)
                lag[i, c] = (mine[c, at] + mates[c, at]).astype(lag.dtype)

                @pl.when(jnp.logical_or(x != tm, x != i))
                def _():
                    row_result(c, i, pair).start()

                @pl.when(jnp.logical_and(x == tm, x == i))
                def _():
                    from_row[pair, c] = lag[i, c]

                @pl.when(has_before)
                def _():
                    next_result(c, i, pair).start()

    def results_sent(c):
        @pl.when(sums)
        def _():
            for i in range(ROW):

                @pl.when(jnp.logical_or(x != tm, x != i))
                def _():
                    row_result(c, i, pair).wait_send()

                @pl.when(has_before)
                def _():
                    next_result(c, i, pair).wait_send()

        @pl.when(jnp.logical_not(sums))
        def _():
            mate_send(c).wait_send()

    @pl.when(jnp.logical_not(has_before))
    def _():
        @pl.loop(0, CHUNKS)
        def _(c):
            up[c] = jnp.zeros(up.shape[1:], up.dtype)

    @pl.when(jnp.logical_not(has_after))
    def _():
        @pl.loop(0, CHUNKS)
        def _(c):
            down[c] = jnp.zeros(down.shape[1:], down.dtype)

    def x_start(u, half):
        for d in (2, 1, 3):
            x_send(u, half, d).start()

    early = PIECES // 2 + 1
    whiten(0, 0)
    pl.semaphore_wait(barrier, peers)
    for u in range(early):
        x_start(u, 0)
    whiten(0, 1)
    for u in range(early):
        x_start(u, 1)
    for u in range(early, PIECES):
        for half in range(2):
            x_start(u, half)
    inv_copy.wait()

    @pl.loop(0, UNITS + USE)
    def _(u):
        @pl.when(u < UNITS)
        def _():
            for half in range(2):
                for d in range(1, ROW):
                    x_send(u, half, d).wait_recv()
            halo_start(u)

        ahead = u // PIECES + 1
        part = lax.rem(u, PIECES)

        @pl.when(jnp.logical_and(ahead < CHUNKS, part < 2))
        def _():
            whiten(ahead, part)

        @pl.when(jnp.logical_and(ahead < CHUNKS, part == 1))
        def _():
            for p in range(PIECES):
                for half in range(2):
                    x_start(ahead * PIECES + p, half)

        @pl.when(jnp.logical_and(u >= PASS, u < UNITS + PASS))
        def _():
            pass_on(u - PASS)

        @pl.when(u >= USE)
        def _():
            k = u - USE
            c, p = k // PIECES, lax.rem(k, PIECES)
            halo_arrived(k)
            correlate(c, p)
            for half in range(2):
                for d in range(1, ROW):
                    x_send(k, half, d).wait_send()
            halo_sent(k)

            @pl.when(p == PIECES - 1)
            def _():
                keep_results(c)

            @pl.when(jnp.logical_and(p == 0, c > 0))
            def _():
                send_results(c - 1)

    send_results(CHUNKS - 1)
    for c in range(CHUNKS):
        for t in range(TM // 2):

            @pl.when(jnp.logical_or(x != tm, pair != t))
            def _():
                row_result(c, 0, t).wait_recv()

            @pl.when(jnp.logical_and(has_after, x < 2))
            def _():
                next_result(c, 0, t).wait_recv()

            @pl.when(jnp.logical_and(has_after, x >= 2))
            def _():
                next_result(c, 2, t).wait_recv()

        for offset in range(1, REACH + 1):
            within = jnp.logical_or(sub < 4, x + offset < ROW)
            at = pl.ds((offset - 1) * 8, 8)
            terms = [
                jnp.where(within, from_row[t, c, at].astype(F32), from_next[t, c, at].astype(F32))
                for t in range(TM // 2)
            ]
            out_ref[offset - 1, 8 * c : 8 * c + 8] = terms[0] + terms[1]
    for c in range(CHUNKS):
        results_sent(c)


def body(records, partners):
    channels, windows, length = records.shape
    total_windows = windows * lax.axis_size("tm")
    scale = 1.0 / math.sqrt(total_windows * FREQ)
    dma = pltpu.SemaphoreType.DMA
    lagged = pl.pallas_call(
        functools.partial(kernel, scale),
        out_shape=jax.ShapeDtypeStruct((REACH, channels // TM, LAGS), F32),
        in_specs=[pl.BlockSpec(memory_space=pl.ANY)] * 3,
        out_specs=pl.BlockSpec(memory_space=pltpu.VMEM),
        scratch_shapes=[
            pltpu.VMEM((CHUNKS, ROW, 2, 4, windows, length), BF16),
            pltpu.VMEM((PIECES, LEN, 2 * WIDE), BF16),
            pltpu.VMEM((PIECES, 2 * WIDE, 2 * LAGS), BF16),
            pltpu.VMEM((ROW, CHUNKS, PIECES, 2, 32, 2 * WIDE), BF16),
            pltpu.VMEM((CHUNKS, PIECES, 2, ROW, 32, 2 * WIDE), BF16),
            pltpu.VMEM((CHUNKS, PIECES, ROW, 32, 2 * WIDE), BF16),
            pltpu.VMEM((CHUNKS, PIECES, ROW, 32, 2 * WIDE), BF16),
            pltpu.VMEM((CHUNKS, PIECES, 2, 32, 2 * WIDE), BF16),
            pltpu.VMEM((128, 2 * WIDE), F32),
            pltpu.VMEM((128, LAGS), F32),
            pltpu.VMEM((CHUNKS, 128, LAGS), F32),
            pltpu.VMEM((CHUNKS, 128, LAGS), F32),
            pltpu.VMEM((ROW, CHUNKS, 32, LAGS), RESULT),
            pltpu.VMEM((TM // 2, CHUNKS, 32, LAGS), RESULT),
            pltpu.VMEM((TM // 2, CHUNKS, 32, LAGS), RESULT),
            dma((CHUNKS,)), dma((PIECES,)), dma,
            dma((UNITS, 2, 3)), dma((UNITS, 2, 3)),
            dma((UNITS, 2, 2)), dma((UNITS, 2, 2)),
            dma((UNITS,)), dma((UNITS,)),
            dma((CHUNKS,)), dma((CHUNKS,)),
            dma((ROW, CHUNKS, 2)), dma((TM // 2, CHUNKS, 2)),
        ],
        compiler_params=pltpu.CompilerParams(
            collective_id=0, has_side_effects=True, vmem_limit_bytes=56 << 20
        ),
        cost_estimate=pl.CostEstimate(
            flops=7 * 10**9, bytes_accessed=12 * 10**6, transcendentals=10**6
        ),
    )(
        records.reshape(ROW, CHUNKS, 2, channels // (ROW * CHUNKS * 2), windows, length),
        jnp.asarray(forward_matrix()),
        jnp.asarray(inverse_matrix()),
    )
    offsets = partners[0] - lax.axis_index("chan")
    chosen = 0.0
    for k in range(REACH):
        chosen = chosen + jnp.where((offsets == k + 1)[:, None, None], lagged[k][None], 0.0)
    return chosen[None]


def solution(mesh):
    return jax.shard_map(
        body,
        mesh=mesh,
        in_specs=(P("chan", "tm", None), P("chan", None)),
        out_specs=P("chan", None, "tm", None),
        check_vma=False,
    )
```

time: 110 us -> 71.3 us (0.65); the launches traced: 108 us -> 71.2 us
  Pallas kernels: 106 us -> 69.6 us
    pallas_call x1, Pallas kernels: 106 us -> 69.6 us  [body(): pl.pallas_call(functools.partial(kernel, scale), out_shape=jax.ShapeDtype...]
where the time goes in v2:
time: 71.3 us; the launch traced here: 71.2 us
  Pallas kernels  69.6 us (98%)
  local copies, waits for them, and re-layouts  0.78 us (1%)
  other arithmetic  0.74 us (1%)
    pallas_call x1, Pallas kernels, body(): pl.pallas_call(functools.partial(kernel, scale), out_shape=jax.ShapeDtype...  69.6 us

profile of v2, /device:TPU:95, one launch (start us, length us, event | category | flops | bytes accessed | tf_op | source)
XLA Modules:
  0.0 71.2 jit_solution(14255543668670472246)
XLA Ops:
  0.0 0.0 copy-start
  0.0 69.6 %shard_map.46 = f32[4,32,128]{2,1,0:T(8,128)} custom-call(bf16[4,4,2,4,8,1920]{5,4,3,2,1,0:T(8,128)(2,1)} %bitcast.17, bf16[3,1920,512]{2,1,0:T(8,128)(2,1)} %constant.20.clone.fwd_hbm, bf16[3,512,256]{2,1,0:T(8,128)(2,1)} %constant.21.clone.inv_hbm), custom_call_target="tpu_custom_call" | custom-call | flops 7000000000 | bytes 12000000 | tf_op jit(solution)/shard_map/pallas_call | solution.py:478
  69.6 0.8 %slice_bitcast_fusion.3 = (f32[32,128]{1,0:T(8,128)S(1)}, f32[32,128]{1,0:T(8,128)S(1)}, f32[32,128]{1,0:T(8,128)S(1)}, f32[32,128]{1,0:T(8,128)S(1)}) fusion(f32[4,32,128]{2,1,0:T(8,128)} %shard_map.46), kind=kLoop, calls=%fused_computation.4 | loop fusion | bytes 131072 | tf_op jit(solution)/shard_map/jit(_where)/broadcast_in_dim | solution.py:520
  70.4 0.0 copy-done
  70.4 0.7 %select_add_fusion = f32[1,4,32,128]{3,2,1,0:T(8,128)} fusion(f32[32,128]{1,0:T(8,128)S(1)} %get-tuple-element.8, f32[32,128]{1,0:T(8,128)S(1)} %get-tuple-element.9, f32[32,128]{1,0:T(8,128)S(1)} %get-tuple-element.10, f32[32,128]{1,0:T(8,128)S(1)} %get-tuple-element.7, pred[4]{0:T(512)(128)(4,1)S(1)} %get-tuple-element.13, ...), kind=kLoop, calls=%fused_computation | loop fusion | flops 114688 | bytes 131088 | tf_op jit(solution)/shard_map/add | solution.py:520
  (2 shorter events, 0.0 us)
Async XLA Ops:
  0.0 70.4 %copy-start = (s32[1,4]{1,0:T(1,128)S(1)}, s32[1,4]{1,0:T(1,128)}, u32[]{:S(2)}) copy-start(s32[1,4]{1,0:T(1,128)} %param.5) | copy-start | bytes 52

commit v3 on v2

--- a/solution.py
+++ b/solution.py
@@ -18,7 +18,7 @@
 CHUNKS = 4
 PIECES = 3
 UNITS = CHUNKS * PIECES
-PASS, USE = 1, 4
+PASS, USE = 2, 5
 WIDE = FREQ // PIECES
 MESH = pl.DeviceIdType.MESH
 F32 = jnp.float32
@@ -74,8 +74,7 @@
     mate = tm + 1 - 2 * core
     sums = lax.rem(x + tm, 2) == 0
     first, last = y == 0, y == ROW - 1
-    passes_down = jnp.logical_and(last, plane > 0)
-    passes_up = jnp.logical_and(first, plane < planes - 1)
+    low, high = plane > 0, plane < planes - 1
 
     def device(by, at=x):
         return lax.rem(row + rows + by, rows) * ROW + at
@@ -112,123 +111,164 @@
     def _():
         greet(chan, mate)
 
-    @pl.when(has_before)
+    @pl.when(jnp.logical_not(first))
     def _():
         greet(device(-1), tm)
 
-        @pl.when(first)
-        def _():
-            greet(device(-ROW), tm)
+    @pl.when(jnp.logical_not(last))
+    def _():
+        greet(device(1), tm)
 
     @pl.when(has_after)
     def _():
-        greet(device(1), tm)
         for t in range(TM // 2):
             greet(device(1, tm), 2 * t + core)
 
-        @pl.when(last)
-        def _():
-            greet(device(ROW), tm)
-
-    @pl.when(passes_up)
-    def _():
-        greet(device(ROW - 1), tm)
-
-    @pl.when(passes_down)
-    def _():
-        greet(device(1 - ROW), tm)
+    for at_edge, near in ((first, ROW - 1), (last, 1 - ROW)):
+        for there, far in ((low, -ROW), (high, ROW)):
+
+            @pl.when(jnp.logical_and(at_edge, there))
+            def _():
+                greet(device(near), tm)
+                greet(device(far), tm)
 
     itself = 1 - ((x - tm) * (x - tm) + 15) // 16
-    before, after = (row + rows - 1) // rows, 1 - (row + 1) // rows
+    before = (row + rows - 1) // rows
     edge = ((2 * y - 3) * (2 * y - 3)) // 9
     around = (plane + planes - 1) // planes + 1 - (plane + 1) // planes
     other = lax.rem(x + tm, 2)
     results = other + (1 - other) * (ROW - itself + ROW * before)
-    peers = ROW - 1 + results + before + after + edge * around
-
-    def x_send(u, half, d):
+    peers = ROW - 1 + results + 2 - edge + 2 * edge * around
+
+    def x_send(u, d, half=None):
         c, p = u // PIECES, lax.rem(u, PIECES)
         there = lax.rem(x + d, ROW)
-        return pltpu.make_async_remote_copy(
-            src_ref=own.at[there, c, p, half], dst_ref=held.at[c, p, half, x],
-            send_sem=xs_sem.at[u, half, d - 1], recv_sem=xr_sem.at[u, half, d - 1],
+        at = (c, p) if half is None else (c, p, half)
+        to = held.at[c, p, :, x] if half is None else held.at[c, p, half, x]
+        return pltpu.make_async_remote_copy(
+            src_ref=own.at[there, *at], dst_ref=to, send_sem=xs_sem, recv_sem=xr_sem.at[u],
             device_id=(device(0, there), tm), device_id_type=MESH,
         )
 
-    def straight(u, half, part):
+    def x_arrived(u):
+        part = held.at[u // PIECES, lax.rem(u, PIECES), :, pl.ds(0, ROW - 1)]
+        pltpu.make_async_remote_copy(
+            src_ref=part, dst_ref=part, send_sem=xs_sem, recv_sem=xr_sem.at[u],
+            device_id=(device(0, lax.rem(x + 1, ROW)), tm), device_id_type=MESH,
+        ).wait_recv()
+
+    def x_sent():
+        part = own.at[pl.ds(0, ROW - 1)]
+        pltpu.make_async_remote_copy(
+            src_ref=part, dst_ref=part, send_sem=xs_sem, recv_sem=xr_sem.at[0],
+            device_id=(device(0, lax.rem(x + 1, ROW)), tm), device_id_type=MESH,
+        ).wait_send()
+
+    def straight(u, half):
         c, p = u // PIECES, lax.rem(u, PIECES)
-        at = pl.ds(2 * part, 2)
-        return pltpu.make_async_remote_copy(
-            src_ref=held.at[c, p, half, at], dst_ref=(up if half else down).at[c, p, at],
-            send_sem=ys_sem.at[u, half, part], recv_sem=yr_sem.at[u, half, part],
+        return pltpu.make_async_remote_copy(
+            src_ref=held.at[c, p, half], dst_ref=(up if half else down).at[c, p],
+            send_sem=ys_sem.at[half], recv_sem=yr_sem.at[u, half],
             device_id=(device(1 if half else -1), tm), device_id_type=MESH,
         )
 
-    def detour(u, half):
+    def cross_y(u, half):
         c, p = u // PIECES, lax.rem(u, PIECES)
         return pltpu.make_async_remote_copy(
-            src_ref=held.at[c, p, half, pl.ds(2, 2)], dst_ref=relay.at[c, p],
-            send_sem=ys_sem.at[u, half, 1], recv_sem=rr_sem.at[u],
+            src_ref=held.at[c, p, half, pl.ds(2, 2)], dst_ref=relay.at[1, c, p],
+            send_sem=ys_sem.at[half], recv_sem=rr_sem.at[u, 1],
             device_id=(device(1 - ROW if half else ROW - 1), tm), device_id_type=MESH,
         )
 
-    def passed_on(u, half):
+    def cross_z(u, half):
         c, p = u // PIECES, lax.rem(u, PIECES)
         return pltpu.make_async_remote_copy(
-            src_ref=relay.at[c, p], dst_ref=(up if half else down).at[c, p, pl.ds(2, 2)],
-            send_sem=rs_sem.at[u], recv_sem=yr_sem.at[u, half, 1],
+            src_ref=held.at[c, p, half, pl.ds(0, 2)], dst_ref=relay.at[0, c, p],
+            send_sem=ys_sem.at[half], recv_sem=rr_sem.at[u, 0],
             device_id=(device(ROW if half else -ROW), tm), device_id_type=MESH,
         )
 
-    sends = ((0, has_before, first), (1, has_after, last))
-    passes = ((0, passes_down), (1, passes_up))
+    def then_z(u, half):
+        c, p = u // PIECES, lax.rem(u, PIECES)
+        return pltpu.make_async_remote_copy(
+            src_ref=relay.at[1, c, p], dst_ref=(up if half else down).at[c, p, pl.ds(2, 2)],
+            send_sem=rs_sem.at[1], recv_sem=yr_sem.at[u, half],
+            device_id=(device(ROW if half else -ROW), tm), device_id_type=MESH,
+        )
+
+    def then_y(u, half):
+        c, p = u // PIECES, lax.rem(u, PIECES)
+        return pltpu.make_async_remote_copy(
+            src_ref=relay.at[0, c, p], dst_ref=(up if half else down).at[c, p, pl.ds(0, 2)],
+            send_sem=rs_sem.at[0], recv_sem=yr_sem.at[u, half],
+            device_id=(device(1 - ROW if half else ROW - 1), tm), device_id_type=MESH,
+        )
+
+    down_here, up_here = jnp.logical_not(first), jnp.logical_not(last)
+    inner = ((0, down_here), (1, up_here))
+    edges = ((0, jnp.logical_and(first, low)), (1, jnp.logical_and(last, high)))
+    turns_z = ((0, jnp.logical_and(last, low)), (1, jnp.logical_and(first, high)))
+    turns_y = ((0, jnp.logical_and(first, high)), (1, jnp.logical_and(last, low)))
 
     def halo_start(u):
-        for half, wanted, at_edge in sends:
-
-            @pl.when(jnp.logical_and(wanted, at_edge))
-            def _():
-                detour(u, half).start()
-
-        for half, wanted, at_edge in sends:
+        for half, wanted in edges:
 
             @pl.when(wanted)
             def _():
-                straight(u, half, 0).start()
-
-            @pl.when(jnp.logical_and(wanted, jnp.logical_not(at_edge)))
-            def _():
-                straight(u, half, 1).start()
+                cross_z(u, half).start()
+                cross_y(u, half).start()
+
+        for half, wanted in inner:
+
+            @pl.when(wanted)
+            def _():
+                straight(u, half).start()
 
     def pass_on(u):
-        for half, wanted in passes:
+        for half, wanted in turns_z:
 
             @pl.when(wanted)
             def _():
-                detour(u, half).wait_recv()
-                passed_on(u, half).start()
+                cross_y(u, half).wait_recv()
+                then_z(u, half).start()
+
+        for half, wanted in turns_y:
+
+            @pl.when(wanted)
+            def _():
+                cross_z(u, half).wait_recv()
+                then_y(u, half).start()
 
     def halo_arrived(u):
         for half, wanted in ((0, has_after), (1, has_before)):
 
             @pl.when(wanted)
             def _():
-                for part in range(2):
-                    straight(u, half, part).wait_recv()
-
-    def halo_sent(u):
-        for half, wanted, _ in sends:
+                straight(u, half).wait_recv()
+
+    def halo_sent():
+        for half, wanted in ((0, has_before), (1, has_after)):
+            whole = up if half else down
 
             @pl.when(wanted)
             def _():
-                for part in range(2):
-                    straight(u, half, part).wait_send()
-
-        for half, wanted in passes:
-
-            @pl.when(wanted)
-            def _():
-                passed_on(u, half).wait_send()
+                pltpu.make_async_remote_copy(
+                    src_ref=whole, dst_ref=whole, send_sem=ys_sem.at[half],
+                    recv_sem=yr_sem.at[0, half],
+                    device_id=(device(1 if half else -1), tm), device_id_type=MESH,
+                ).wait_send()
+
+        for part, turns in ((1, turns_z), (0, turns_y)):
+            for half, wanted in turns:
+                whole = relay.at[part]
+
+                @pl.when(wanted)
+                def _():
+                    pltpu.make_async_remote_copy(
+                        src_ref=whole, dst_ref=whole, send_sem=rs_sem.at[part],
+                        recv_sem=yr_sem.at[0, half],
+                        device_id=(device(1 if half else -1), tm), device_id_type=MESH,
+                    ).wait_send()
 
     def mate_send(c):
         return pltpu.make_async_remote_copy(
@@ -240,7 +280,7 @@
     def row_result(c, i, t):
         return pltpu.make_async_remote_copy(
             src_ref=lag.at[i, c], dst_ref=from_row.at[t, c],
-            send_sem=os_sem.at[i, c, 0], recv_sem=or_sem.at[t, c, 0],
+            send_sem=os_sem.at[c, 0], recv_sem=or_sem.at[c, 0],
             device_id=(device(0, i), x), device_id_type=MESH,
         )
 
@@ -248,7 +288,7 @@
         at = pl.ds(16, 16) if i < 2 else pl.ds(0, 32)
         return pltpu.make_async_remote_copy(
             src_ref=lag.at[i, c, at], dst_ref=from_next.at[t, c, at],
-            send_sem=os_sem.at[i, c, 1], recv_sem=or_sem.at[t, c, 1],
+            send_sem=os_sem.at[c, 1], recv_sem=or_sem.at[c, 1],
             device_id=(device(-1, i), x), device_id_type=MESH,
         )
 
@@ -351,22 +391,47 @@
                 def _():
                     next_result(c, i, pair).start()
 
+    def results_wait(c, kind, part):
+        return pltpu.make_async_remote_copy(
+            src_ref=part, dst_ref=part, send_sem=os_sem.at[c, kind], recv_sem=or_sem.at[c, kind],
+            device_id=(device(-1 if kind else 0, x), x), device_id_type=MESH,
+        )
+
     def results_sent(c):
         @pl.when(sums)
         def _():
-            for i in range(ROW):
-
-                @pl.when(jnp.logical_or(x != tm, x != i))
-                def _():
-                    row_result(c, i, pair).wait_send()
-
-                @pl.when(has_before)
-                def _():
-                    next_result(c, i, pair).wait_send()
+            @pl.when(x != tm)
+            def _():
+                results_wait(c, 0, lag.at[:, c]).wait_send()
+
+            @pl.when(x == tm)
+            def _():
+                results_wait(c, 0, lag.at[pl.ds(0, ROW - 1), c]).wait_send()
+
+            @pl.when(has_before)
+            def _():
+                results_wait(c, 1, lag.at[pl.ds(0, ROW - 1), c]).wait_send()
 
         @pl.when(jnp.logical_not(sums))
         def _():
             mate_send(c).wait_send()
+
+    def results_arrived(c):
+        @pl.when(x != tm)
+        def _():
+            results_wait(c, 0, from_row.at[:, c]).wait_recv()
+
+        @pl.when(x == tm)
+        def _():
+            results_wait(c, 0, from_row.at[pl.ds(0, 1), c]).wait_recv()
+
+        @pl.when(jnp.logical_and(has_after, x < 2))
+        def _():
+            results_wait(c, 1, from_next.at[:, c, pl.ds(16, 16)]).wait_recv()
+
+        @pl.when(jnp.logical_and(has_after, x >= 2))
+        def _():
+            results_wait(c, 1, from_next.at[:, c]).wait_recv()
 
     @pl.when(jnp.logical_not(has_before))
     def _():
@@ -380,9 +445,9 @@
         def _(c):
             down[c] = jnp.zeros(down.shape[1:], down.dtype)
 
-    def x_start(u, half):
+    def x_start(u, half=None):
         for d in (2, 1, 3):
-            x_send(u, half, d).start()
+            x_send(u, d, half).start()
 
     early = PIECES // 2 + 1
     whiten(0, 0)
@@ -393,31 +458,26 @@
     for u in range(early):
         x_start(u, 1)
     for u in range(early, PIECES):
-        for half in range(2):
-            x_start(u, half)
+        x_start(u)
     inv_copy.wait()
 
     @pl.loop(0, UNITS + USE)
     def _(u):
         @pl.when(u < UNITS)
         def _():
-            for half in range(2):
-                for d in range(1, ROW):
-                    x_send(u, half, d).wait_recv()
+            x_arrived(u)
             halo_start(u)
 
-        ahead = u // PIECES + 1
-        part = lax.rem(u, PIECES)
-
-        @pl.when(jnp.logical_and(ahead < CHUNKS, part < 2))
+        ahead, part = u // 2 + 1, lax.rem(u, 2)
+
+        @pl.when(ahead < CHUNKS)
         def _():
             whiten(ahead, part)
 
         @pl.when(jnp.logical_and(ahead < CHUNKS, part == 1))
         def _():
             for p in range(PIECES):
-                for half in range(2):
-                    x_start(ahead * PIECES + p, half)
+                x_start(ahead * PIECES + p)
 
         @pl.when(jnp.logical_and(u >= PASS, u < UNITS + PASS))
         def _():
@@ -429,10 +489,6 @@
             c, p = k // PIECES, lax.rem(k, PIECES)
             halo_arrived(k)
             correlate(c, p)
-            for half in range(2):
-                for d in range(1, ROW):
-                    x_send(k, half, d).wait_send()
-            halo_sent(k)
 
             @pl.when(p == PIECES - 1)
             def _():
@@ -443,21 +499,10 @@
                 send_results(c - 1)
 
     send_results(CHUNKS - 1)
+    x_sent()
+    halo_sent()
     for c in range(CHUNKS):
-        for t in range(TM // 2):
-
-            @pl.when(jnp.logical_or(x != tm, pair != t))
-            def _():
-                row_result(c, 0, t).wait_recv()
-
-            @pl.when(jnp.logical_and(has_after, x < 2))
-            def _():
-                next_result(c, 0, t).wait_recv()
-
-            @pl.when(jnp.logical_and(has_after, x >= 2))
-            def _():
-                next_result(c, 2, t).wait_recv()
-
+        results_arrived(c)
         for offset in range(1, REACH + 1):
             within = jnp.logical_or(sub < 4, x + offset < ROW)
             at = pl.ds((offset - 1) * 8, 8)
@@ -488,7 +533,7 @@
             pltpu.VMEM((CHUNKS, PIECES, 2, ROW, 32, 2 * WIDE), BF16),
             pltpu.VMEM((CHUNKS, PIECES, ROW, 32, 2 * WIDE), BF16),
             pltpu.VMEM((CHUNKS, PIECES, ROW, 32, 2 * WIDE), BF16),
-            pltpu.VMEM((CHUNKS, PIECES, 2, 32, 2 * WIDE), BF16),
+            pltpu.VMEM((2, CHUNKS, PIECES, 2, 32, 2 * WIDE), BF16),
             pltpu.VMEM((128, 2 * WIDE), F32),
             pltpu.VMEM((128, LAGS), F32),
             pltpu.VMEM((CHUNKS, 128, LAGS), F32),
@@ -497,11 +542,11 @@
             pltpu.VMEM((TM // 2, CHUNKS, 32, LAGS), RESULT),
             pltpu.VMEM((TM // 2, CHUNKS, 32, LAGS), RESULT),
             dma((CHUNKS,)), dma((PIECES,)), dma,
-            dma((UNITS, 2, 3)), dma((UNITS, 2, 3)),
-            dma((UNITS, 2, 2)), dma((UNITS, 2, 2)),
-            dma((UNITS,)), dma((UNITS,)),
+            dma, dma((UNITS,)),
+            dma((2,)), dma((UNITS, 2)),
+            dma((2,)), dma((UNITS, 2)),
             dma((CHUNKS,)), dma((CHUNKS,)),
-            dma((ROW, CHUNKS, 2)), dma((TM // 2, CHUNKS, 2)),
+            dma((CHUNKS, 2)), dma((CHUNKS, 2)),
         ],
         compiler_params=pltpu.CompilerParams(
             collective_id=0, has_side_effects=True, vmem_limit_bytes=56 << 20

time: 71.3 us -> 67.5 us (0.947); the launches traced: 71.2 us -> 66.2 us
  Pallas kernels: 69.6 us -> 64.6 us
    pallas_call x1, Pallas kernels: 69.6 us -> 64.6 us  [body(): pl.pallas_call(functools.partial(kernel, scale), out_shape=jax.ShapeDtype...]
where the time goes in v3:
time: 67.5 us; the launch traced here: 66.2 us
  Pallas kernels  64.6 us (96%)
  local copies, waits for them, and re-layouts  0.78 us (1%)
  other arithmetic  0.74 us (1%)
    pallas_call x1, Pallas kernels, body(): pl.pallas_call(functools.partial(kernel, scale), out_shape=jax.ShapeDtype...  64.6 us

profile of v3, /device:TPU:95, one launch (start us, length us, event | category | flops | bytes accessed | tf_op | source)
XLA Modules:
  0.0 66.2 jit_solution(17892176710007827121)
XLA Ops:
  0.0 0.0 copy-start
  0.0 64.6 %shard_map.46 = f32[4,32,128]{2,1,0:T(8,128)} custom-call(bf16[4,4,2,4,8,1920]{5,4,3,2,1,0:T(8,128)(2,1)} %bitcast.17, bf16[3,1920,512]{2,1,0:T(8,128)(2,1)} %constant.20.clone.fwd_hbm, bf16[3,512,256]{2,1,0:T(8,128)(2,1)} %constant.21.clone.inv_hbm), custom_call_target="tpu_custom_call" | custom-call | flops 7000000000 | bytes 12000000 | tf_op jit(solution)/shard_map/pallas_call | solution.py:523
  64.6 0.8 %slice_bitcast_fusion.3 = (f32[32,128]{1,0:T(8,128)S(1)}, f32[32,128]{1,0:T(8,128)S(1)}, f32[32,128]{1,0:T(8,128)S(1)}, f32[32,128]{1,0:T(8,128)S(1)}) fusion(f32[4,32,128]{2,1,0:T(8,128)} %shard_map.46), kind=kLoop, calls=%fused_computation.4 | loop fusion | bytes 131072 | tf_op jit(solution)/shard_map/jit(_where)/broadcast_in_dim | solution.py:565
  65.4 0.0 copy-done
  65.5 0.7 %select_add_fusion = f32[1,4,32,128]{3,2,1,0:T(8,128)} fusion(f32[32,128]{1,0:T(8,128)S(1)} %get-tuple-element.8, f32[32,128]{1,0:T(8,128)S(1)} %get-tuple-element.9, f32[32,128]{1,0:T(8,128)S(1)} %get-tuple-element.10, f32[32,128]{1,0:T(8,128)S(1)} %get-tuple-element.7, pred[4]{0:T(512)(128)(4,1)S(1)} %get-tuple-element.13, ...), kind=kLoop, calls=%fused_computation | loop fusion | flops 114688 | bytes 131088 | tf_op jit(solution)/shard_map/add | solution.py:565
  (2 shorter events, 0.0 us)
Async XLA Ops:
  0.0 65.4 %copy-start = (s32[1,4]{1,0:T(1,128)S(1)}, s32[1,4]{1,0:T(1,128)}, u32[]{:S(2)}) copy-start(s32[1,4]{1,0:T(1,128)} %param.5) | copy-start | bytes 52

commit v4 on v3

--- a/solution.py
+++ b/solution.py
@@ -89,9 +89,6 @@
     for p in range(PIECES):
         fwd_copy(p).start()
     inv_copy = pltpu.make_async_copy(inv_hbm, inv, inv_sem)
-    inv_copy.start()
-    for c in range(1, CHUNKS):
-        rec_copy(c).start()
 
     from_next[...] = jnp.zeros(from_next.shape, from_next.dtype)
     barrier = pltpu.get_barrier_semaphore()
@@ -451,6 +448,9 @@
 
     early = PIECES // 2 + 1
     whiten(0, 0)
+    inv_copy.start()
+    for c in range(1, CHUNKS):
+        rec_copy(c).start()
     pl.semaphore_wait(barrier, peers)
     for u in range(early):
         x_start(u, 0)
@@ -468,6 +468,10 @@
             x_arrived(u)
             halo_start(u)
 
+        @pl.when(jnp.logical_and(u >= PASS, u < UNITS + PASS))
+        def _():
+            pass_on(u - PASS)
+
         ahead, part = u // 2 + 1, lax.rem(u, 2)
 
         @pl.when(ahead < CHUNKS)
@@ -478,10 +482,6 @@
         def _():
             for p in range(PIECES):
                 x_start(ahead * PIECES + p)
-
-        @pl.when(jnp.logical_and(u >= PASS, u < UNITS + PASS))
-        def _():
-            pass_on(u - PASS)
 
         @pl.when(u >= USE)
         def _():

time: 67.5 us -> 65.9 us (0.976)
  Pallas kernels: 64.6 us -> 63.5 us
    pallas_call x1, Pallas kernels: 64.6 us -> 63.5 us  [body(): pl.pallas_call(functools.partial(kernel, scale), out_shape=jax.ShapeDtype...]
where the time goes in v4:
time: 65.9 us; the launch traced here: 65 us
  Pallas kernels  63.5 us (96%)
  local copies, waits for them, and re-layouts  0.78 us (1%)
  other arithmetic  0.74 us (1%)
    pallas_call x1, Pallas kernels, body(): pl.pallas_call(functools.partial(kernel, scale), out_shape=jax.ShapeDtype...  63.5 us

profile of v4, /device:TPU:95, one launch (start us, length us, event | category | flops | bytes accessed | tf_op | source)
XLA Modules:
  0.0 65.0 jit_solution(11812388994834147406)
XLA Ops:
  0.0 0.0 copy-start
  0.0 63.5 %shard_map.46 = f32[4,32,128]{2,1,0:T(8,128)} custom-call(bf16[4,4,2,4,8,1920]{5,4,3,2,1,0:T(8,128)(2,1)} %bitcast.17, bf16[3,1920,512]{2,1,0:T(8,128)(2,1)} %constant.20.clone.fwd_hbm, bf16[3,512,256]{2,1,0:T(8,128)(2,1)} %constant.21.clone.inv_hbm), custom_call_target="tpu_custom_call" | custom-call | flops 7000000000 | bytes 12000000 | tf_op jit(solution)/shard_map/pallas_call | solution.py:523
  63.5 0.8 %slice_bitcast_fusion.3 = (f32[32,128]{1,0:T(8,128)S(1)}, f32[32,128]{1,0:T(8,128)S(1)}, f32[32,128]{1,0:T(8,128)S(1)}, f32[32,128]{1,0:T(8,128)S(1)}) fusion(f32[4,32,128]{2,1,0:T(8,128)} %shard_map.46), kind=kLoop, calls=%fused_computation.4 | loop fusion | bytes 131072 | tf_op jit(solution)/shard_map/jit(_where)/broadcast_in_dim | solution.py:565
  64.2 0.0 copy-done
  64.3 0.7 %select_add_fusion = f32[1,4,32,128]{3,2,1,0:T(8,128)} fusion(f32[32,128]{1,0:T(8,128)S(1)} %get-tuple-element.8, f32[32,128]{1,0:T(8,128)S(1)} %get-tuple-element.9, f32[32,128]{1,0:T(8,128)S(1)} %get-tuple-element.10, f32[32,128]{1,0:T(8,128)S(1)} %get-tuple-element.7, pred[4]{0:T(512)(128)(4,1)S(1)} %get-tuple-element.13, ...), kind=kLoop, calls=%fused_computation | loop fusion | flops 114688 | bytes 131088 | tf_op jit(solution)/shard_map/add | solution.py:565
  (2 shorter events, 0.0 us)
Async XLA Ops:
  0.0 64.2 %copy-start = (s32[1,4]{1,0:T(1,128)S(1)}, s32[1,4]{1,0:T(1,128)}, u32[]{:S(2)}) copy-start(s32[1,4]{1,0:T(1,128)} %param.5) | copy-start | bytes 52

commit v5 on v4

--- a/solution.py
+++ b/solution.py
@@ -503,14 +503,13 @@
     halo_sent()
     for c in range(CHUNKS):
         results_arrived(c)
+        inside = from_row[0, c].astype(F32) + from_row[1, c].astype(F32)
+        beyond = from_next[0, c].astype(F32) + from_next[1, c].astype(F32)
         for offset in range(1, REACH + 1):
             within = jnp.logical_or(sub < 4, x + offset < ROW)
-            at = pl.ds((offset - 1) * 8, 8)
-            terms = [
-                jnp.where(within, from_row[t, c, at].astype(F32), from_next[t, c, at].astype(F32))
-                for t in range(TM // 2)
-            ]
-            out_ref[offset - 1, 8 * c : 8 * c + 8] = terms[0] + terms[1]
+            at = (offset - 1) * 8
+            tile = jnp.where(within, inside[at : at + 8], beyond[at : at + 8])
+            out_ref[offset - 1, 8 * c : 8 * c + 8] = tile
     for c in range(CHUNKS):
         results_sent(c)
 

time: 65.9 us -> 65.9 us (level)
  no operation moved by 1% of the time
where the time goes in v5:
time: 65.9 us; the launch traced here: 65 us
  Pallas kernels  63.5 us (96%)
  local copies, waits for them, and re-layouts  0.78 us (1%)
  other arithmetic  0.74 us (1%)
    pallas_call x1, Pallas kernels, body(): pl.pallas_call(functools.partial(kernel, scale), out_shape=jax.ShapeDtype...  63.5 us

profile of v5, /device:TPU:95, one launch (start us, length us, event | category | flops | bytes accessed | tf_op | source)
XLA Modules:
  0.0 65.0 jit_solution(13718935140409358973)
XLA Ops:
  0.0 0.0 copy-start
  0.0 63.5 %shard_map.46 = f32[4,32,128]{2,1,0:T(8,128)} custom-call(bf16[4,4,2,4,8,1920]{5,4,3,2,1,0:T(8,128)(2,1)} %bitcast.17, bf16[3,1920,512]{2,1,0:T(8,128)(2,1)} %constant.20.clone.fwd_hbm, bf16[3,512,256]{2,1,0:T(8,128)(2,1)} %constant.21.clone.inv_hbm), custom_call_target="tpu_custom_call" | custom-call | flops 7000000000 | bytes 12000000 | tf_op jit(solution)/shard_map/pallas_call | solution.py:522
  63.5 0.8 %slice_bitcast_fusion.3 = (f32[32,128]{1,0:T(8,128)S(1)}, f32[32,128]{1,0:T(8,128)S(1)}, f32[32,128]{1,0:T(8,128)S(1)}, f32[32,128]{1,0:T(8,128)S(1)}) fusion(f32[4,32,128]{2,1,0:T(8,128)} %shard_map.46), kind=kLoop, calls=%fused_computation.4 | loop fusion | bytes 131072 | tf_op jit(solution)/shard_map/jit(_where)/broadcast_in_dim | solution.py:564
  64.2 0.0 copy-done
  64.3 0.7 %select_add_fusion = f32[1,4,32,128]{3,2,1,0:T(8,128)} fusion(f32[32,128]{1,0:T(8,128)S(1)} %get-tuple-element.8, f32[32,128]{1,0:T(8,128)S(1)} %get-tuple-element.9, f32[32,128]{1,0:T(8,128)S(1)} %get-tuple-element.10, f32[32,128]{1,0:T(8,128)S(1)} %get-tuple-element.7, pred[4]{0:T(512)(128)(4,1)S(1)} %get-tuple-element.13, ...), kind=kLoop, calls=%fused_computation | loop fusion | flops 114688 | bytes 131088 | tf_op jit(solution)/shard_map/add | solution.py:564
  (2 shorter events, 0.0 us)
Async XLA Ops:
  0.0 64.2 %copy-start = (s32[1,4]{1,0:T(1,128)S(1)}, s32[1,4]{1,0:T(1,128)}, u32[]{:S(2)}) copy-start(s32[1,4]{1,0:T(1,128)} %param.5) | copy-start | bytes 52

commit v6 on v5

--- a/solution.py
+++ b/solution.py
@@ -13,6 +13,7 @@
 LAGS = 128
 REACH = 4
 LEN = 1920
+HALF, DEEP = LEN // 2, 1024
 ROW = 4
 TM = 4
 CHUNKS = 4
@@ -26,20 +27,26 @@
 RESULT = jnp.bfloat16
 
 
+def bin_order():
+    return np.concatenate([np.arange(2, FREQ + 1, 2), np.arange(1, FREQ + 1, 2)]).astype(np.int64)
+
+
 def forward_matrix():
-    times = np.arange(LEN, dtype=np.int64)[:, None]
-    bins = np.arange(1, FREQ + 1, dtype=np.int64)[None, :]
+    times = np.arange(HALF, dtype=np.int64)[:, None]
+    bins = bin_order()[None, :]
     angle = 2.0 * math.pi / LEN * (times * bins % LEN)
     real, imag = np.cos(angle), -np.sin(angle)
     pieces = [
         np.concatenate([real[:, p * WIDE : (p + 1) * WIDE], imag[:, p * WIDE : (p + 1) * WIDE]], 1)
         for p in range(PIECES)
     ]
-    return np.stack(pieces).astype(np.float32).astype(BF16)
+    table = np.zeros((PIECES, DEEP, 2 * WIDE), np.float32)
+    table[:, :HALF] = np.stack(pieces)
+    return table.astype(BF16)
 
 
 def inverse_matrix():
-    bins = np.arange(1, FREQ + 1, dtype=np.int64)[:, None]
+    bins = bin_order()[:, None]
     shifts = np.arange(LAGS, dtype=np.int64)[None, :] - LAGS // 2
     angle = 2.0 * math.pi / LEN * (bins * shifts % LEN)
     whole = np.concatenate([np.cos(angle), -np.sin(angle)], 0).astype(np.float32)
@@ -295,12 +302,20 @@
             rec_copy(c).wait()
 
         data = rec[c, :, half].reshape(128, LEN)
+        second = pltpu.roll(data[:, LEN - DEEP :], HALF, 1)
+        data = jnp.concatenate([data[:, :DEEP], second], axis=0)
         reals, imags, mags = [], [], []
         for p in range(PIECES):
             if isinstance(c, int) and c == 0 and half == 0:
                 fwd_copy(p).wait()
             spectrum = jnp.dot(data, fwd[p], preferred_element_type=F32)
-            real, imag = spectrum[:, :WIDE], spectrum[:, WIDE:]
+            columns = []
+            for at in range(0, 2 * WIDE, 128):
+                before, after = spectrum[:128, at : at + 128], spectrum[128:, at : at + 128]
+                even = 2 * (p * WIDE + at % WIDE) < FREQ
+                columns.append(before + after if even else before - after)
+            real = jnp.concatenate(columns[: WIDE // 128], axis=1)
+            imag = jnp.concatenate(columns[WIDE // 128 :], axis=1)
             reals.append(real)
             imags.append(imag)
             mags.append(jnp.sqrt(real * real + imag * imag))
@@ -526,7 +541,7 @@
         out_specs=pl.BlockSpec(memory_space=pltpu.VMEM),
         scratch_shapes=[
             pltpu.VMEM((CHUNKS, ROW, 2, 4, windows, length), BF16),
-            pltpu.VMEM((PIECES, LEN, 2 * WIDE), BF16),
+            pltpu.VMEM((PIECES, DEEP, 2 * WIDE), BF16),
             pltpu.VMEM((PIECES, 2 * WIDE, 2 * LAGS), BF16),
             pltpu.VMEM((ROW, CHUNKS, PIECES, 2, 32, 2 * WIDE), BF16),
             pltpu.VMEM((CHUNKS, PIECES, 2, ROW, 32, 2 * WIDE), BF16),

time: 65.9 us -> 65.8 us (level)
  no operation moved by 1% of the time
where the time goes in v6:
time: 65.8 us; the launch traced here: 64.7 us
  Pallas kernels  63.1 us (96%)
  local copies, waits for them, and re-layouts  0.78 us (1%)
  other arithmetic  0.74 us (1%)
    pallas_call x1, Pallas kernels, body(): pl.pallas_call(functools.partial(kernel, scale), out_shape=jax.ShapeDtype...  63.1 us

profile of v6, /device:TPU:95, one launch (start us, length us, event | category | flops | bytes accessed | tf_op | source)
XLA Modules:
  0.0 64.7 jit_solution(13995962334045249260)
XLA Ops:
  0.0 0.0 copy-start
  0.0 63.1 %shard_map.46 = f32[4,32,128]{2,1,0:T(8,128)} custom-call(bf16[4,4,2,4,8,1920]{5,4,3,2,1,0:T(8,128)(2,1)} %bitcast.17, bf16[3,1024,512]{2,1,0:T(8,128)(2,1)} %constant.20.clone.fwd_hbm, bf16[3,512,256]{2,1,0:T(8,128)(2,1)} %constant.21.clone.inv_hbm), custom_call_target="tpu_custom_call" | custom-call | flops 7000000000 | bytes 12000000 | tf_op jit(solution)/shard_map/pallas_call | solution.py:537
  63.1 0.8 %slice_bitcast_fusion.3 = (f32[32,128]{1,0:T(8,128)S(1)}, f32[32,128]{1,0:T(8,128)S(1)}, f32[32,128]{1,0:T(8,128)S(1)}, f32[32,128]{1,0:T(8,128)S(1)}) fusion(f32[4,32,128]{2,1,0:T(8,128)} %shard_map.46), kind=kLoop, calls=%fused_computation.4 | loop fusion | bytes 131072 | tf_op jit(solution)/shard_map/jit(_where)/broadcast_in_dim | solution.py:579
  63.9 0.0 copy-done
  64.0 0.7 %select_add_fusion = f32[1,4,32,128]{3,2,1,0:T(8,128)} fusion(f32[32,128]{1,0:T(8,128)S(1)} %get-tuple-element.8, f32[32,128]{1,0:T(8,128)S(1)} %get-tuple-element.9, f32[32,128]{1,0:T(8,128)S(1)} %get-tuple-element.10, f32[32,128]{1,0:T(8,128)S(1)} %get-tuple-element.7, pred[4]{0:T(512)(128)(4,1)S(1)} %get-tuple-element.13, ...), kind=kLoop, calls=%fused_computation | loop fusion | flops 114688 | bytes 131088 | tf_op jit(solution)/shard_map/add | solution.py:579
  (2 shorter events, 0.0 us)
Async XLA Ops:
  0.0 63.9 %copy-start = (s32[1,4]{1,0:T(1,128)S(1)}, s32[1,4]{1,0:T(1,128)}, u32[]{:S(2)}) copy-start(s32[1,4]{1,0:T(1,128)} %param.5) | copy-start | bytes 52
